TPU v7x, 256 devices: a whole 4x4x8 slice. The times are simulated.
256 devices in a mesh: fsdp: 32 (over z, y_hi, core), tp: 8 (over y_lo, x).
Axes of the slice: x: 4, y: 4 (y_hi: 2, y_lo: 2; y = y_hi * 2 + y_lo), z: 8, core: 2. Of those that a mesh axis runs over, the one named last changes fastest.
Arguments:
- train_x: bfloat16 [32768, 8192], P('fsdp'), may hold values from -6 to 6
- train_q: bfloat16 [32768, 8192], P('fsdp', 'tp'), may hold values from -17 to 17
- train_k: bfloat16 [32768, 1024], P('fsdp', 'tp'), may hold values from -14 to 14
- train_target: bfloat16 [32768, 8192], P('fsdp', 'tp'), may hold values from -6 to 6
- train_skill: int32 [128], replicated, may hold values from 0 to 3, as said below
- value_weight: bfloat16 [8192, 1024], P('fsdp', 'tp'), may hold values from -0.0625 to 0.0625
- val_x: bfloat16 [4096, 8192], P('fsdp'), may hold values from -6 to 6
- val_q: bfloat16 [4096, 8192], P('fsdp', 'tp'), may hold values from -17 to 17
- val_k: bfloat16 [4096, 1024], P('fsdp', 'tp'), may hold values from -14 to 14
- val_target: bfloat16 [4096, 8192], P('fsdp', 'tp'), may hold values from -6 to 6
- val_skill: int32 [32], replicated, may hold values from 0 to 3, as said below
Outputs:
- skill_grads: bfloat16 [4, 8192, 1024], P(None, 'fsdp', 'tp')
- transfer: float32 [4, 4], replicated
Inputs may be any that keep to these rules, and one draw needn't show every extreme that they name: `train_skill`: each of the 4 skills labels exactly 32 sequences. `val_skill`: each of the 4 skills labels exactly 8 sequences.
All inputs are finite; a program needn't handle non-finite values.
Results may differ from a plain program's by a relative error of at most 0.0052.
The roundings to bfloat16 on the way count: a program that leaves them out, or rounds other values in their place, can miss the bound.
Values may be sent and summed in bfloat16 or wider, within the bound.
No kernel may reach another device: no remote copies, remote signals or barrier semaphores. Data moves between devices by JAX's collectives and lax.ppermute only.
A program may use at most 192 MiB of HBM per device.

v0:
```python
import math
import jax
import jax.numpy as jnp
from jax import lax
from jax.sharding import PartitionSpec as P

HD = 128
SKILLS = 4
SEQ = 256
VSEQ = 128
step_size = 0.01


def attend(query_rows, key_rows, length):
    members = query_rows.shape[0] // length
    kv_heads = key_rows.shape[1] // HD
    group = query_rows.shape[1] // HD // kv_heads
    queries = query_rows.reshape(members, length, kv_heads, group, HD)
    keys = key_rows.reshape(members, length, kv_heads, HD)
    scores = jnp.einsum("bqgrh,bkgh->bgrqk", queries, keys, preferred_element_type=jnp.float32) * (
        1.0 / math.sqrt(HD)
    )
    places = jnp.arange(length)
    allowed = places[:, None] >= places[None, :]
    scores = jnp.where(allowed, scores, jnp.float32(-1e30))
    highest = jnp.max(scores, axis=-1, keepdims=True)
    raised = jnp.exp(scores - highest)
    return (raised / jnp.sum(raised, axis=-1, keepdims=True)).astype(jnp.bfloat16)


def on_device(
    train_x,
    train_q,
    train_k,
    train_target,
    train_skill,
    value_weight,
    val_x,
    val_q,
    val_k,
    val_target,
    val_skill,
):
    head_width = train_k.shape[1]
    kv_heads = head_width // HD
    group = train_q.shape[1] // head_width
    train_rows = train_x.shape[0]
    val_rows = val_x.shape[0]
    train_members = train_rows // SEQ
    val_members = val_rows // VSEQ
    skill_ids = jnp.arange(SKILLS, dtype=jnp.int32)
    shard_rows = lax.all_gather(value_weight, "fsdp", axis=0, tiled=True)
    values = jnp.dot(train_x, shard_rows, preferred_element_type=jnp.float32)
    val_values = jnp.dot(val_x, shard_rows, preferred_element_type=jnp.float32)
    values = values.astype(jnp.bfloat16)
    val_values = val_values.astype(jnp.bfloat16)
    attention = attend(train_q, train_k, SEQ)
    value_blocks = values.reshape(train_members, SEQ, kv_heads, HD)
    mixed = jnp.einsum(
        "bgrqk,bkgh->bqgrh", attention, value_blocks, preferred_element_type=jnp.float32
    )
    target_blocks = train_target.reshape(train_members, SEQ, kv_heads, group, HD).astype(
        jnp.float32
    )
    residual = ((mixed - target_blocks) / SEQ).astype(jnp.bfloat16)
    value_grads = jnp.einsum(
        "bgrqk,bqgrh->bkgh", attention, residual, preferred_element_type=jnp.float32
    )
    grad_rows = value_grads.reshape(train_rows, head_width).astype(jnp.bfloat16)
    train_first = lax.axis_index("fsdp") * train_members
    local_skill = lax.dynamic_slice_in_dim(train_skill, train_first, train_members)
    local_indicator = (local_skill[:, None] == skill_ids[None, :]).astype(jnp.float32)
    running = jnp.zeros(
        (lax.axis_size("fsdp") * (train_x.shape[1] // lax.axis_size("fsdp")), SKILLS, head_width),
        jnp.float32,
    )
    for sequence in range(train_members):
        product = jnp.dot(
            train_x[sequence * SEQ : (sequence + 1) * SEQ].T,
            grad_rows[sequence * SEQ : (sequence + 1) * SEQ],
            preferred_element_type=jnp.float32,
        )
        running = running + local_indicator[sequence][None, :, None] * product[:, None, :]
    shares = lax.psum_scatter(running, "fsdp", scatter_dimension=0, tiled=True)
    skill_grads = jnp.transpose(shares, (1, 0, 2)).astype(jnp.bfloat16)
    val_attention = attend(val_q, val_k, VSEQ)
    val_blocks = val_values.reshape(val_members, VSEQ, kv_heads, HD)
    val_mixed = jnp.einsum(
        "bgrqk,bkgh->bqgrh", val_attention, val_blocks, preferred_element_type=jnp.float32
    )
    val_target_blocks = val_target.reshape(val_members, VSEQ, kv_heads, group, HD).astype(
        jnp.float32
    )
    val_residual = (val_mixed - val_target_blocks) / VSEQ
    val_pull = jnp.einsum(
        "bgrqk,bqgrh->bkgh",
        val_attention.astype(jnp.float32),
        val_residual,
        precision=lax.Precision.HIGHEST,
    )
    val_pull = val_pull.reshape(val_rows, head_width)
    tangent = jnp.einsum(
        "td,sdc->tsc",
        val_x,
        lax.all_gather(skill_grads, "fsdp", axis=1, tiled=True),
        preferred_element_type=jnp.float32,
    )
    along = jnp.einsum("tsc,tc->ts", tangent, val_pull, precision=lax.Precision.HIGHEST)
    val_first = lax.axis_index("fsdp") * val_members
    val_local = lax.dynamic_slice_in_dim(val_skill, val_first, val_members)
    val_indicator = jnp.repeat(
        (val_local[:, None] == skill_ids[None, :]).astype(jnp.float32), VSEQ, axis=0
    )
    partial_transfer = step_size * jnp.dot(along.T, val_indicator, precision=lax.Precision.HIGHEST)
    transfer = lax.psum(partial_transfer, ("fsdp", "tp"))
    return (skill_grads, transfer)


def solution(mesh):
    placed = (
        P("fsdp", None),
        P("fsdp", "tp"),
        P("fsdp", "tp"),
        P("fsdp", "tp"),
        P(),
        P("fsdp", "tp"),
        P("fsdp", None),
        P("fsdp", "tp"),
        P("fsdp", "tp"),
        P("fsdp", "tp"),
        P(),
    )
    return jax.shard_map(
        on_device,
        mesh=mesh,
        in_specs=placed,
        out_specs=(P(None, "fsdp", "tp"), P()),
        check_vma=False,
    )
```

profile of v0, /device:TPU:1, one launch (start us, length us, event | category | flops | bytes accessed | tf_op | source)
XLA Modules:
  0.0 577.4 jit_solution(3521864218452400355)
XLA Ops:
  7.2 0.0 copy-start
  7.2 0.0 all-gather.3.cloned.1.call-start
  7.2 0.7 all-gather.3.cloned.1.call-update
  7.9 0.0 reduce-scatter.2.cloned.1.call-start
  8.0 3.6 copy.56
  11.5 2.0 convert_bitcast_fusion
  13.6 0.0 copy-start.6
  13.6 0.0 copy-start.4
  13.6 2.9 copy.57
  16.5 5.2 copy.28
  21.8 0.0 copy-done.6
  21.8 0.1 dynamic_slice.6
  21.9 0.1 fusion.66
  22.0 0.0 copy-done.4
  22.0 3.1 fusion.1
  25.0 0.0 copy-start.1
  25.0 3.2 copy-done.1
  28.2 1.9 fusion
  30.1 64.9 %all-gather.3.cloned.1.call-done = bf16[8192,128]{1,0:T(8,128)(2,1)} async-done(((bf16[256,128]{1,0:T(8,128)(2,1)}), bf16[8192,128]{1,0:T(8,128)(2,1)}) %all-gather.3.cloned.1.call-update) | async-done | bytes 2097168 | tf_op jit(solution)/shard_map/all_gather | solution.py:52
  95.0 10.8 %convolution_convert_fusion = bf16[1024,128]{1,0:T(8,128)(2,1)S(1)} fusion(bf16[1024,8192]{1,0:T(8,128)(2,1)} %param.11, bf16[8192,128]{1,0:T(8,128)(2,1)} %all-gather.3.cloned.1.call-done), kind=kOutput, calls=%fused_computation.35 | convolution fusion | flops 2147614720 | bytes 19136512 | tf_op jit(solution)/shard_map/dot_general | solution.py:53
  105.9 9.5 %fusion.42 = bf16[4,256,1,128]{1,3,0,2:T(8,128)(2,1)S(1)} fusion(f32[4,8,256]{2,1,0:T(8,128)S(1)} %fusion, f32[4,8,256]{2,1,0:T(8,128)S(1)} %get-tuple-element.6, f32[4,256,256,8]{2,1,3,0:T(8,128)} %copy-done.1, pred[256,256]{0,1:T(8,128)(4,1)S(1)} %iota_compare_fusion, f32[4,256,1,8,128]{1,4,3,0,2:T(8,128)} %copy.28, bf16[4,256,128,1]{2,1,3,0:T(8,128)(2,1)S(1)} %bitcast.216), kind=kOutput, calls=%fused_computation.38 | convolution fusion | flops 1097990144 | bytes 13238272 | tf_op jit(solution)/shard_map/bgrqk,bqgrh->bkgh/dot_general | solution.py:66
  115.4 4.9 convolution_bitcast_fusion
  120.3 4.9 convolution_bitcast_fusion.1
  125.2 4.9 convolution_bitcast_fusion.2
  130.1 4.8 convolution_bitcast_fusion.3
  134.9 5.6 copy.33
  140.5 5.6 copy.32
  146.1 5.6 copy.31
  151.6 5.6 copy.30
  157.2 12.5 %multiply_add_fusion = f32[8192,4,128]{2,0,1:T(8,128)} fusion(f32[8192,128]{1,0:T(8,128)} %copy.33, f32[4]{0:T(128)S(1)} %get-tuple-element.3, f32[8192,128]{1,0:T(8,128)} %copy.32, f32[4]{0:T(128)S(1)} %get-tuple-element.4, f32[8192,128]{1,0:T(8,128)} %copy.31, f32[4]{0:T(128)S(1)} %get-tuple-element.5, f32[8192,128]{1,0:T(8,128)} %copy.30, ...), kind=kLoop, calls=%fused_computation | loop fusion | flops 29360128 | bytes 33554496 | tf_op jit(solution)/shard_map/add | solution.py:83
  169.8 0.0 copy-start.5
  169.8 0.0 reduce-scatter.2.cloned.1.call-update
  169.8 0.0 all-gather.5.cloned.1.call-start
  169.9 212.2 %reduce-scatter.2.cloned.1.call-done = f32[256,4,128]{2,0,1:T(8,128)} async-done(((f32[8192,4,128]{2,0,1:T(8,128)}), f32[256,4,128]{2,0,1:T(8,128)}) %reduce-scatter.2.cloned.1.call-update) | async-done | bytes 524304 | tf_op jit(solution)/shard_map/reduce_scatter | solution.py:84
  382.1 1.8 convert_bitcast_fusion.1
  383.9 0.0 all-gather.5.cloned.1.call-update
  383.9 0.0 copy-done.2
  383.9 0.1 copy.36
  384.1 0.6 dynamic_slice.7
  384.7 0.6 compare_convert_fusion
  385.3 0.2 fusion.72
  385.6 0.1 fusion.59
  385.7 3.5 fusion.33
  389.2 1.5 convolution_bitcast_fusion.5
  390.7 99.5 %all-gather.5.cloned.1.call-done = bf16[4,8192,128]{2,1,0:T(8,128)(2,1)} async-done(((bf16[4,256,128]{2,1,0:T(8,128)(2,1)}), bf16[4,8192,128]{2,1,0:T(8,128)(2,1)}) %all-gather.5.cloned.1.call-update) | async-done | bytes 8388624 | tf_op jit(solution)/shard_map/all_gather | solution.py:105
  490.2 5.8 fusion.55
  495.9 0.2 convolution_multiply_fusion.1
  496.1 74.7 %psum.7 = f32[4,4]{1,0:T(4,128)} all-reduce(f32[4,4]{1,0:T(4,128)S(1)} %convolution_multiply_fusion.1), channel_id=1, replica_groups=mesh['fsdp'=32,'tp'=8] {'fsdp','tp'}, use_global_device_ids=true, to_apply=%region_5.6 | all-reduce | flops 16 | bytes 128 | tf_op jit(solution)/shard_map/psum | solution.py:115
  (10 shorter events, 0.1 us)
Async XLA Ops:
  7.2 378.5 %copy-start = (bf16[128,8192]{1,0:T(8,128)(2,1)S(1)}, bf16[128,8192]{1,0:T(8,128)(2,1)}, u32[]{:S(2)}) copy-start(bf16[128,8192]{1,0:T(8,128)(2,1)} %param.17) | copy-start | bytes 6291460
  7.2 87.8 %all-gather.3.cloned.1.call-start = ((), (), s32[]{:S(2)}) async-start(), calls=%async_computation.1 | async-start | bytes 2162688 | tf_op jit(solution)/shard_map/all_gather | solution.py:52
  7.9 374.2 %reduce-scatter.2.cloned.1.call-start = ((), (), s32[]{:S(2)}) async-start(), calls=%async_computation.2 | async-start | bytes 17301504 | tf_op jit(solution)/shard_map/reduce_scatter | solution.py:84
  13.6 8.2 %copy-start.6 = (s32[128]{0:T(128)S(1)}, s32[128]{0:T(128)}, u32[]{:S(2)}) copy-start(s32[128]{0:T(128)} %param.15) | copy-start | bytes 1540
  13.6 8.4 %copy-start.4 = (bf16[1024,128]{1,0:T(8,128)(2,1)S(1)}, bf16[1024,128]{1,0:T(8,128)(2,1)}, u32[]{:S(2)}) copy-start(bf16[1024,128]{1,0:T(8,128)(2,1)} %param.13) | copy-start | bytes 786436
  25.0 3.2 copy-start.1
  169.8 214.1 %copy-start.2 = (bf16[128,1024]{1,0:T(8,128)(2,1)S(1)}, bf16[128,1024]{1,0:T(8,128)(2,1)}, u32[]{:S(2)}) copy-start(bf16[128,1024]{1,0:T(8,128)(2,1)} %param.20) | copy-start | bytes 786436
  169.8 214.3 %copy-start.7 = (s32[32]{0:T(128)S(1)}, s32[32]{0:T(128)}, u32[]{:S(2)}) copy-start(s32[32]{0:T(128)} %param.21) | copy-start | bytes 388
  169.8 215.5 %copy-start.3 = (bf16[128,1024]{1,0:T(8,128)(2,1)S(1)}, bf16[128,1024]{1,0:T(8,128)(2,1)}, u32[]{:S(2)}) copy-start(bf16[128,1024]{1,0:T(8,128)(2,1)} %param.18) | copy-start | bytes 786436
  169.8 215.6 %copy-start.5 = (bf16[128,128]{1,0:T(8,128)(2,1)S(1)}, bf16[128,128]{1,0:T(8,128)(2,1)}, u32[]{:S(2)}) copy-start(bf16[128,128]{1,0:T(8,128)(2,1)} %param.19) | copy-start | bytes 98308
  169.8 320.4 %all-gather.5.cloned.1.call-start = ((), (), s32[]{:S(2)}) async-start(), calls=%async_computation.3 | async-start | bytes 8650752 | tf_op jit(solution)/shard_map/all_gather | solution.py:105
Sparse Core Ops, SparseCore 0:
  10.8 84.1 all-gather.2
  169.9 212.1 reduce-scatter.1
  385.9 104.2 all-gather.4
where the time goes:
time: 578 us; the launch traced here: 577 us
  waiting for transfers between devices  377 us (65%)
  blocking collectives  74.7 us (13%)
  matrix products  54.1 us (9%)
  local copies, waits for them, and re-layouts  38.1 us (7%)
  other arithmetic  19.1 us (3%)
  between operations  13.9 us (2%)
    reduce_scatter x1, waiting for transfers between devices, on_device(): shares = lax.psum_scatter(running, 'fsdp', scatter_dimension=0, tiled=True)  212 us
    all_gather x1, waiting for transfers between devices, on_device(): lax.all_gather(skill_grads, 'fsdp', axis=1, tiled=True)  99.5 us
    psum x1, blocking collectives, on_device(): transfer = lax.psum(partial_transfer, ('fsdp', 'tp'))  74.7 us
    all_gather x1, waiting for transfers between devices, on_device(): shard_rows = lax.all_gather(value_weight, 'fsdp', axis=0, tiled=True)  64.9 us
    dot_general x4, local copies, waits for them, and re-layouts, on_device(): jnp.dot(train_x[sequence * SEQ:(sequence + 1) * SEQ].T, grad_rows[sequenc...  22.3 us
    dot_general x4, matrix products, on_device(): jnp.dot(train_x[sequence * SEQ:(sequence + 1) * SEQ].T, grad_rows[sequenc...  19.5 us
    add x1, other arithmetic, on_device(): running + local_indicator[sequence][None, :, None] * product[:, None, :]  12.5 us
  transfers between devices with their start and end apart: 3, of which 3 were waited for; matrix products, arithmetic and copies ran while one was open for 4% of the time, Pallas kernels for 0%

commit v1 on v0

--- a/solution.py
+++ b/solution.py
@@ -112,7 +112,7 @@
         (val_local[:, None] == skill_ids[None, :]).astype(jnp.float32), VSEQ, axis=0
     )
     partial_transfer = step_size * jnp.dot(along.T, val_indicator, precision=lax.Precision.HIGHEST)
-    transfer = lax.psum(partial_transfer, ("fsdp", "tp"))
+    transfer = jnp.sum(lax.all_gather(partial_transfer, ("fsdp", "tp")), axis=0)
     return (skill_grads, transfer)
 
 

time: 578 us -> 1100 us (1.90); the launches traced: 577 us -> 1090 us
  blocking collectives: 74.7 us -> 611 us
  local copies, waits for them, and re-layouts: 38.1 us -> 16.6 us
    all_gather x0 -> x1, blocking collectives: none -> 611 us  [on_device(): transfer = jnp.sum(lax.all_gather(partial_transfer, ('fsdp', 'tp')), axis=0)]
    psum x1 -> x0, blocking collectives: 74.7 us -> none  [on_device(): transfer = lax.psum(partial_transfer, ('fsdp', 'tp'))]
    dot_general x4 -> x0, local copies, waits for them, and re-layouts: 22.3 us -> none  [on_device(): jnp.dot(train_x[sequence * SEQ:(sequence + 1) * SEQ].T, grad_rows[sequenc...]
  transfers between devices with their start and end apart: 3 -> 3, of which waited for: 3 -> 3; matrix products, arithmetic and copies ran while one was open for 4% -> 3% of each run, Pallas kernels for 0% -> 0%
where the time goes in v1:
time: 1100 us; the launch traced here: 1090 us
  blocking collectives  611 us (56%)
  waiting for transfers between devices  382 us (35%)
  matrix products  47 us (4%)
  local copies, waits for them, and re-layouts  16.6 us (2%)
  other arithmetic  14.8 us (1%)
  between operations  13.9 us (1%)
    all_gather x1, blocking collectives, on_device(): transfer = jnp.sum(lax.all_gather(partial_transfer, ('fsdp', 'tp')), axis=0)  611 us
    reduce_scatter x1, waiting for transfers between devices, on_device(): shares = lax.psum_scatter(running, 'fsdp', scatter_dimension=0, tiled=True)  213 us
    all_gather x1, waiting for transfers between devices, on_device(): lax.all_gather(skill_grads, 'fsdp', axis=1, tiled=True)  104 us
    all_gather x1, waiting for transfers between devices, on_device(): shard_rows = lax.all_gather(value_weight, 'fsdp', axis=0, tiled=True)  64.9 us
  transfers between devices with their start and end apart: 3, of which 3 were waited for; matrix products, arithmetic and copies ran while one was open for 3% of the time, Pallas kernels for 0%

profile of v1, /device:TPU:1, one launch (start us, length us, event | category | flops | bytes accessed | tf_op | source)
XLA Modules:
  0.0 1085.5 jit_solution(17230255528998577464)
XLA Ops:
  7.2 0.0 copy-start
  7.2 0.0 all-gather.5.cloned.1.call-start
  7.2 0.7 all-gather.5.cloned.1.call-update
  7.9 0.0 reduce-scatter.2.cloned.1.call-start
  8.0 3.6 copy.69
  11.5 2.0 convert_bitcast_fusion
  13.6 0.0 copy-start.6
  13.6 0.0 copy-start.4
  13.6 2.9 copy.70
  16.5 5.2 copy.41
  21.8 0.0 copy-done.6
  21.8 0.1 dynamic_slice.6
  21.9 0.1 fusion.67
  22.0 0.0 copy-done.4
  22.0 3.1 fusion.1
  25.0 0.0 copy-start.1
  25.0 3.2 copy-done.1
  28.2 1.9 fusion
  30.1 64.9 %all-gather.5.cloned.1.call-done = bf16[8192,128]{1,0:T(8,128)(2,1)} async-done(((bf16[256,128]{1,0:T(8,128)(2,1)}), bf16[8192,128]{1,0:T(8,128)(2,1)}) %all-gather.5.cloned.1.call-update) | async-done | bytes 2097168 | tf_op jit(solution)/shard_map/all_gather | solution.py:52
  95.0 10.8 convolution_convert_fusion
  105.9 9.5 fusion.42
  115.4 2.9 convolution_bitcast_fusion
  118.3 2.9 convolution_bitcast_fusion.1
  121.3 2.9 convolution_bitcast_fusion.2
  124.2 2.9 convolution_bitcast_fusion.3
  127.1 7.4 multiply_add_fusion
  134.5 0.0 reduce-scatter.2.cloned.1.call-update
  134.6 0.0 all-gather.7.cloned.1.call-start
  134.6 212.7 %reduce-scatter.2.cloned.1.call-done = f32[256,4,128]{0,2,1:T(8,128)} async-done(((f32[8192,4,128]{0,2,1:T(8,128)}), f32[256,4,128]{0,2,1:T(8,128)}) %reduce-scatter.2.cloned.1.call-update) | async-done | bytes 524304 | tf_op jit(solution)/shard_map/reduce_scatter | solution.py:84
  347.4 1.8 convert_bitcast_fusion.1
  349.1 0.0 all-gather.7.cloned.1.call-update
  349.2 0.0 copy-done.3
  349.2 0.1 copy.46
  349.3 0.0 copy-done.7
  349.3 0.6 dynamic_slice.7
  349.9 0.6 compare_convert_fusion
  350.6 0.0 copy-done.5
  350.6 1.2 fusion.73
  351.8 0.1 fusion.60
  351.9 3.4 fusion.33
  355.3 1.5 convolution_bitcast_fusion.5
  356.8 0.0 copy-done.2
  356.8 0.8 copy.48
  357.6 103.9 %all-gather.7.cloned.1.call-done = bf16[4,8192,128]{1,2,0:T(8,128)(2,1)} async-done(((bf16[4,256,128]{1,2,0:T(8,128)(2,1)}), bf16[4,8192,128]{1,2,0:T(8,128)(2,1)}) %all-gather.7.cloned.1.call-update) | async-done | bytes 8388624 | tf_op jit(solution)/shard_map/all_gather | solution.py:105
  461.5 5.7 fusion.55
  467.3 0.2 fusion.59
  467.4 610.7 %all-gather.1 = f32[256,4,4]{2,1,0:T(4,128)S(1)} all-gather(f32[1,4,4]{2,1,0:T(4,128)S(1)} %fusion.59), channel_id=2, replica_groups=mesh['fsdp'=32,'tp'=8] {'fsdp','tp'}, dimensions={0}, use_global_device_ids=true | all-gather | bytes 16448 | tf_op jit(solution)/shard_map/all_gather | solution.py:115
  1078.1 0.9 reduce_sum.29
  (8 shorter events, 0.1 us)
Async XLA Ops:
  7.2 344.7 %copy-start = (bf16[128,8192]{1,0:T(8,128)(2,1)S(1)}, bf16[128,8192]{1,0:T(8,128)(2,1)}, u32[]{:S(2)}) copy-start(bf16[128,8192]{1,0:T(8,128)(2,1)} %param.17) | copy-start | bytes 6291460
  7.2 87.8 %all-gather.5.cloned.1.call-start = ((), (), s32[]{:S(2)}) async-start(), calls=%async_computation.1 | async-start | bytes 2162688 | tf_op jit(solution)/shard_map/all_gather | solution.py:52
  7.9 339.4 %reduce-scatter.2.cloned.1.call-start = ((), (), s32[]{:S(2)}) async-start(), calls=%async_computation.2 | async-start | bytes 17301504 | tf_op jit(solution)/shard_map/reduce_scatter | solution.py:84
  13.6 8.2 copy-start.6
  13.6 8.4 copy-start.4
  25.0 3.2 copy-start.1
  134.5 214.6 %copy-start.3 = (bf16[128,1024]{1,0:T(8,128)(2,1)S(1)}, bf16[128,1024]{1,0:T(8,128)(2,1)}, u32[]{:S(2)}) copy-start(bf16[128,1024]{1,0:T(8,128)(2,1)} %param.20) | copy-start | bytes 786436
  134.5 214.8 %copy-start.7 = (s32[32]{0:T(128)S(1)}, s32[32]{0:T(128)}, u32[]{:S(2)}) copy-start(s32[32]{0:T(128)} %param.21) | copy-start | bytes 388
  134.5 216.1 %copy-start.5 = (bf16[128,128]{1,0:T(8,128)(2,1)S(1)}, bf16[128,128]{1,0:T(8,128)(2,1)}, u32[]{:S(2)}) copy-start(bf16[128,128]{1,0:T(8,128)(2,1)} %param.19) | copy-start | bytes 98308
  134.6 327.0 %all-gather.7.cloned.1.call-start = ((), (), s32[]{:S(2)}) async-start(), calls=%async_computation.3 | async-start | bytes 8650752 | tf_op jit(solution)/shard_map/all_gather | solution.py:105
  349.1 7.6 copy-start.2
Sparse Core Ops, SparseCore 0:
  10.8 84.1 all-gather.4
  134.7 212.6 reduce-scatter.1
  350.2 111.2 all-gather.6
